TPU v7x, 128 devices: a whole 4x4x4 slice. The times are simulated.
128 devices in a mesh: fsdp: 8 (over y, x_lo), tp: 16 (over z, x_hi, core).
Axes of the slice: x: 4 (x_hi: 2, x_lo: 2; x = x_hi * 2 + x_lo), y: 4, z: 4, core: 2. Of those that a mesh axis runs over, the one named last changes fastest.
Arguments:
- activ: bfloat16 [2048, 8192], P('tp', 'fsdp'), may hold values from -6 to 6
- policy_gate: bfloat16 [8192, 14336], P(('fsdp', 'tp')), may hold values from -0.0625 to 0.0625
- policy_up: bfloat16 [8192, 14336], P(('fsdp', 'tp')), may hold values from -0.0625 to 0.0625
- policy_down: bfloat16 [14336, 8192], P(None, ('fsdp', 'tp')), may hold values from -0.046875 to 0.046875
- old_gate: bfloat16 [8192, 14336], P(('fsdp', 'tp')), may hold values from -0.0625 to 0.0625
- old_up: bfloat16 [8192, 14336], P(('fsdp', 'tp')), may hold values from -0.0625 to 0.0625
- old_down: bfloat16 [14336, 8192], P(None, ('fsdp', 'tp')), may hold values from -0.046875 to 0.046875
Outputs:
- ffn_out: bfloat16 [2048, 8192], P('tp', 'fsdp')
All inputs are finite; a program needn't handle non-finite values.
Results may differ from a plain program's by a relative error of at most 0.03.
Values may be sent and summed in bfloat16 or wider, within the bound.
A program may use at most 128 MiB of HBM per device.

v0:
```python
import jax
import jax.numpy as jnp
from jax import lax
from jax.sharding import PartitionSpec as P


def blend(policy, older):
    return (0.6 * policy.astype(jnp.float32) + 0.4 * older.astype(jnp.float32)).astype(jnp.bfloat16)


def activate(sums, width):
    return (jax.nn.silu(sums[:, :width]) * sums[:, width:]).astype(jnp.bfloat16)


def per_device(activ, policy_gate, policy_up, policy_down, old_gate, old_up, old_down):
    mixed_gate, mixed_up = (
        lax.all_to_all(blend(policy_gate, old_gate), "tp", split_axis=1, concat_axis=0, tiled=True),
        lax.all_to_all(blend(policy_up, old_up), "tp", split_axis=1, concat_axis=0, tiled=True),
    )
    mixed_down = lax.all_to_all(
        blend(policy_down, old_down), "tp", split_axis=0, concat_axis=1, tiled=True
    )
    width = mixed_gate.shape[1]
    paired = jnp.concatenate([mixed_gate, mixed_up], axis=1)
    partials = jnp.dot(
        lax.all_gather(activ, "tp", axis=0, tiled=True), paired, preferred_element_type=jnp.float32
    )
    share_sums = lax.psum_scatter(
        partials.astype(jnp.bfloat16), "fsdp", scatter_dimension=0, tiled=True
    ).astype(jnp.float32)
    hidden = lax.all_gather(activate(share_sums, width), "fsdp", axis=0, tiled=True)
    return lax.psum_scatter(
        jnp.dot(hidden, mixed_down, preferred_element_type=jnp.float32).astype(jnp.bfloat16),
        "tp",
        scatter_dimension=0,
        tiled=True,
    )


def solution(mesh):
    in_specs = (
        P("tp", "fsdp"),
        P(("fsdp", "tp"), None),
        P(("fsdp", "tp"), None),
        P(None, ("fsdp", "tp")),
        P(("fsdp", "tp"), None),
        P(("fsdp", "tp"), None),
        P(None, ("fsdp", "tp")),
    )
    out_specs = P("tp", "fsdp")
    return jax.shard_map(
        per_device, mesh=mesh, in_specs=in_specs, out_specs=out_specs, check_vma=False
    )
```

profile of v0, /device:TPU:0, one launch (start us, length us, event | category | flops | bytes accessed | tf_op | source)
XLA Modules:
  0.0 451.2 jit_solution(9811498055950554464)
XLA Ops:
  6.5 0.7 all-gather.3.cloned.1.call-update
  7.3 2.7 add_convert_fusion.2
  10.0 1.5 copy.22
  11.5 8.0 %all-to-all-start = ((bf16[64,16,896]{2,0,1:T(8,128)(2,1)}), bf16[64,16,896]{2,0,1:T(8,128)(2,1)}, u32[]{:S(2)}, u32[]{:S(2)}) async-start(bf16[64,16,896]{2,0,1:T(8,128)(2,1)} %bitcast.25), calls=%async_computation | async-start | bytes 3670016 | tf_op jit(solution)/shard_map/all_to_all | solution.py:17
  19.5 0.0 reduce-scatter.3.cloned.1.call-start
  19.6 2.2 add_convert_fusion.1
  21.7 0.3 copy.21
  22.0 26.9 %all-to-all-done = bf16[64,16,896]{2,0,1:T(8,128)(2,1)} async-done(((bf16[64,16,896]{2,0,1:T(8,128)(2,1)}), bf16[64,16,896]{2,0,1:T(8,128)(2,1)}, u32[]{:S(2)}, u32[]{:S(2)}) %all-to-all-start) | async-done | bytes 1835040 | tf_op jit(solution)/shard_map/all_to_all | solution.py:17
  48.9 41.3 %all_to_all.57 = bf16[64,16,896]{2,0,1:T(8,128)(2,1)} all-to-all(bf16[64,16,896]{2,0,1:T(8,128)(2,1)S(1)} %bitcast.26), channel_id=1, replica_groups=mesh['fsdp'=8,'tp'=16] {'tp'}, dimensions={1} | all-to-all | bytes 3670016 | tf_op jit(solution)/shard_map/all_to_all | solution.py:18
  90.2 2.1 all-gather.3.cloned.1.call-done
  92.2 12.6 %fusion = bf16[2048,1792]{0,1:T(8,128)(2,1)} fusion(bf16[2048,1024]{1,0:T(8,128)(2,1)} %all-gather.3.cloned.1.call-done, bf16[1024,896]{1,0:T(8,128)(2,1)} %bitcast.31, bf16[1024,896]{1,0:T(8,128)(2,1)} %bitcast.1), kind=kOutput, calls=%fused_computation.1 | convolution fusion | flops 7527202816 | bytes 15204352 | tf_op jit(solution)/shard_map/dot_general | solution.py:25
  104.9 0.0 reduce-scatter.3.cloned.1.call-update
  104.9 0.0 all-gather.5.cloned.1.call-start
  105.0 147.0 %reduce-scatter.3.cloned.1.call-done = bf16[256,1792]{0,1:T(8,128)(2,1)} async-done(((bf16[2048,1792]{0,1:T(8,128)(2,1)}), bf16[256,1792]{0,1:T(8,128)(2,1)}) %reduce-scatter.3.cloned.1.call-update) | async-done | bytes 917520 | tf_op jit(solution)/shard_map/reduce_scatter | solution.py:28
  251.9 1.3 convert_element_type.50
  253.2 1.0 fusion.4
  254.3 0.0 all-gather.5.cloned.1.call-update
  254.3 0.0 reduce-scatter.5.cloned.1.call-start
  254.4 2.2 add_convert_fusion
  256.5 0.3 copy.20
  256.8 52.5 %all_to_all.58 = bf16[16,896,64]{1,2,0:T(8,128)(2,1)S(1)} all-to-all(bf16[16,896,64]{1,2,0:T(8,128)(2,1)S(1)} %bitcast.27), channel_id=1, replica_groups=mesh['fsdp'=8,'tp'=16] {'tp'}, dimensions={0} | all-to-all | bytes 3670016 | tf_op jit(solution)/shard_map/all_to_all | solution.py:20
  309.2 45.3 %all-gather.5.cloned.1.call-done = bf16[2048,896]{0,1:T(8,128)(2,1)} async-done(((bf16[256,896]{0,1:T(8,128)(2,1)}), bf16[2048,896]{0,1:T(8,128)(2,1)}) %all-gather.5.cloned.1.call-update) | async-done | bytes 3670032 | tf_op jit(solution)/shard_map/all_gather | solution.py:31
  354.5 8.3 %convolution_convert_fusion.1 = bf16[2048,1024]{1,0:T(8,128)(2,1)} fusion(bf16[2048,896]{0,1:T(8,128)(2,1)} %all-gather.5.cloned.1.call-done, bf16[896,1024]{0,1:T(8,128)(2,1)S(1)} %bitcast.32), kind=kOutput, calls=%fused_computation.2 | convolution fusion | flops 3760193536 | bytes 9699328 | tf_op jit(solution)/shard_map/dot_general | solution.py:33
  362.8 81.9 %reduce-scatter.5.cloned.1.call-done = bf16[128,1024]{1,0:T(8,128)(2,1)} async-done(((bf16[2048,1024]{1,0:T(8,128)(2,1)}), bf16[128,1024]{1,0:T(8,128)(2,1)}) %reduce-scatter.5.cloned.1.call-update) | async-done | bytes 262160 | tf_op jit(solution)/shard_map/reduce_scatter | solution.py:32
  (6 shorter events, 0.0 us)
Async XLA Ops:
  6.5 85.7 %all-gather.3.cloned.1.call-start = ((), (), s32[]{:S(2)}) async-start(), calls=%async_computation.5 | async-start | bytes 4456448 | tf_op jit(solution)/shard_map/all_gather | solution.py:26
  10.0 9.6 %copy-start = (bf16[64,14336]{1,0:T(8,128)(2,1)S(1)}, bf16[64,14336]{1,0:T(8,128)(2,1)}, u32[]{:S(2)}) copy-start(bf16[64,14336]{1,0:T(8,128)(2,1)} %param.12) | copy-start | bytes 5505028
  11.5 37.4 %all-to-all-start = ((bf16[64,16,896]{2,0,1:T(8,128)(2,1)}), bf16[64,16,896]{2,0,1:T(8,128)(2,1)}, u32[]{:S(2)}, u32[]{:S(2)}) async-start(bf16[64,16,896]{2,0,1:T(8,128)(2,1)} %bitcast.25), calls=%async_computation | async-start | bytes 3670016 | tf_op jit(solution)/shard_map/all_to_all | solution.py:17
  19.5 232.4 %reduce-scatter.3.cloned.1.call-start = ((), (), s32[]{:S(2)}) async-start(), calls=%async_computation.6 | async-start | bytes 8257536 | tf_op jit(solution)/shard_map/reduce_scatter | solution.py:28
  104.9 149.5 %copy-start.1 = (bf16[14336,64]{0,1:T(8,128)(2,1)S(1)}, bf16[14336,64]{0,1:T(8,128)(2,1)}, u32[]{:S(2)}) copy-start(bf16[14336,64]{0,1:T(8,128)(2,1)} %param.13) | copy-start | bytes 5505028
  104.9 249.6 %all-gather.5.cloned.1.call-start = ((), (), s32[]{:S(2)}) async-start(), calls=%async_computation.7 | async-start | bytes 4128768 | tf_op jit(solution)/shard_map/all_gather | solution.py:31
  254.3 190.4 %reduce-scatter.5.cloned.1.call-start = ((), (), s32[]{:S(2)}) async-start(), calls=%async_computation.8 | async-start | bytes 4456448 | tf_op jit(solution)/shard_map/reduce_scatter | solution.py:32
Sparse Core Ops, SparseCore 0:
  9.8 82.3 all-gather.2
  105.0 146.8 reduce-scatter.2
  254.4 100.0 all-gather.4
  362.9 81.6 reduce-scatter.4
where the time goes:
time: 452 us; the launch traced here: 451 us
  waiting for transfers between devices  304 us (67%)
  blocking collectives  93.7 us (21%)
  matrix products  20.9 us (5%)
  between operations  13.2 us (3%)
  other arithmetic  9.36 us (2%)
  starting transfers between devices  8.13 us (2%)
    reduce_scatter x1, waiting for transfers between devices, per_device(): lax.psum_scatter(partials.astype(jnp.bfloat16), 'fsdp', scatter_dimension...  147 us
    reduce_scatter x1, waiting for transfers between devices, per_device(): lax.psum_scatter(jnp.dot(hidden, mixed_down, preferred_element_type=jnp.f...  81.9 us
    all_to_all x1, blocking collectives, per_device(): lax.all_to_all(blend(policy_down, old_down), 'tp', split_axis=0, concat_a...  52.5 us
    all_gather x1, waiting for transfers between devices, per_device(): lax.all_gather(activate(share_sums, width), 'fsdp', axis=0, tiled=True)  45.3 us
    all_to_all x1, blocking collectives, per_device(): lax.all_to_all(blend(policy_up, old_up), 'tp', split_axis=1, concat_axis=...  41.3 us
    all_to_all x1, waiting for transfers between devices, per_device(): lax.all_to_all(blend(policy_gate, old_gate), 'tp', split_axis=1, concat_a...  26.9 us
    dot_general x1, matrix products, per_device(): jnp.dot(lax.all_gather(activ, 'tp', axis=0, tiled=True), paired, preferre...  12.6 us
  transfers between devices with their start and end apart: 5, of which 5 were waited for; matrix products, arithmetic and copies ran while one was open for 2% of the time, Pallas kernels for 0%

commit v1 on v0

v1 whole, which is shorter than its diff:
```python
import functools

import jax
import jax.numpy as jnp
from jax import lax
from jax.experimental import pallas as pl
from jax.experimental.pallas import tpu as pltpu
from jax.sharding import PartitionSpec as P

MESH = pl.DeviceIdType.MESH
F32, BF16 = jnp.float32, jnp.bfloat16

SIDE = 4
CHIPS = 16
ROWS = 64
UNITS = 896
PLANE = 2048
TOKENS = 2048
QUARTER = 512
BLOCK = 128
FEATS = 1024
CHUNKS = ((0, 256), (256, 256), (512, 384))


def device(x, y, z, c):
    return (y * 2 + x % 2, z * 4 + (x // 2) * 2 + c)


def shift(v, d):
    return lax.rem(v + d, SIDE)


def wait_bytes(ref, sem):
    pltpu.make_async_copy(ref, ref, sem).wait()


def mixed(a, b):
    return (0.6 * a.astype(F32) + 0.4 * b.astype(F32)).astype(BF16)


def kernel(
    act_in, pg_in, pu_in, pd_in, og_in, ou_in, od_in, out,
    mix, old, act, wbuf, dbuf, part, rs, xs, xr, hid, ob, o1, o2s, o2,
    ld, act_ss, act_rs, act_fs, w_ss, w_rs, d_ss, d_rs, d_fs,
    r_ss, r_rs, x_ss, x_rs, h_ss, h_rs, o1_ss, o1_rs, o2_ss, o2_rs,
):
    f, t = lax.axis_index("fsdp"), lax.axis_index("tp")
    y, x_lo = f // 2, lax.rem(f, 2)
    z, x_hi, c = t // 4, lax.rem(t // 2, 2), lax.rem(t, 2)
    x = x_hi * 2 + x_lo
    first = c == 0
    chip = z * SIDE + x
    sibling = device(x, y, z, 1 - c)

    def send(src, dst, send_sem, recv_sem, to):
        pltpu.make_async_remote_copy(
            src_ref=src, dst_ref=dst, send_sem=send_sem, recv_sem=recv_sem, device_id=to, device_id_type=MESH
        ).start()

    def act_block(xx, zz, cc):
        tok = (zz * 4 + (xx // 2) * 2 + cc) * BLOCK
        return act.at[pl.ds(pl.multiple_of(tok, BLOCK), BLOCK), pl.ds(pl.multiple_of(lax.rem(xx, 2) * FEATS, FEATS), FEATS)]

    def weight_rows(xx, zz, cc):
        row = lax.rem(xx, 2) * FEATS + (zz * 2 + xx // 2) * 128 + cc * ROWS
        return pl.ds(pl.multiple_of(row, ROWS), ROWS)

    loads = [
        pltpu.make_async_copy(a, b, ld.at[i])
        for i, (a, b) in enumerate(
            [
                (act_in, act_block(x, z, c)),
                (pg_in, mix.at[0]), (og_in, old.at[0]),
                (pu_in, mix.at[1]), (ou_in, old.at[1]),
                (pd_in, mix.at[2]), (od_in, old.at[2]),
            ]
        )
    ]
    for copy in loads:
        copy.start()

    barrier = pltpu.get_barrier_semaphore()

    def greet(i, carry):
        to = device(shift(x, lax.rem(i // 2, 4)), y, shift(z, i // 8), lax.rem(c + i, 2))
        pl.semaphore_signal(barrier, inc=1, device_id=to, device_id_type=MESH)
        return carry

    lax.fori_loop(1, 32, greet, 0)
    for d in (1, 2, 3):
        pl.semaphore_signal(barrier, inc=1, device_id=device(x, shift(y, d), z, c), device_id_type=MESH)
    pl.semaphore_wait(barrier, 34)

    def along_a(d):
        return jnp.where(first, shift(x, d), x), jnp.where(first, z, shift(z, d))

    def along_b(d):
        return jnp.where(first, x, shift(x, d)), jnp.where(first, shift(z, d), z)

    def block_of(da, db):
        return jnp.where(first, shift(x, da), shift(x, db)), jnp.where(first, shift(z, db), shift(z, da))

    def send_block(xx, zz, to_x, to_z):
        ref = act_block(xx, zz, c)
        send(ref, ref, act_ss, act_rs.at[zz * SIDE + xx], device(to_x, y, to_z, c))

    def share_block(xx, zz):
        ref = act_block(xx, zz, c)
        send(ref, ref, act_ss, act_fs, sibling)

    loads[0].wait()
    for d in (1, 3, 2):
        send_block(x, z, *along_a(d))
    share_block(x, z)

    def send_weights(k):
        c0, cw = CHUNKS[k]
        target = wbuf.at[weight_rows(x, z, c), pl.ds(c0, cw)]

        def blend(p):
            cols = pl.ds(pl.multiple_of(p * UNITS + c0, 128), cw)
            for m in (0, 1):
                mix[m, :, cols] = mixed(mix[m, :, cols], old[m, :, cols])
            return cols

        own = blend(chip)
        pltpu.make_async_copy(mix.at[c, :, own], target, w_rs.at[k]).start()
        send(mix.at[1 - c, :, own], target, w_ss.at[k], w_rs.at[k], sibling)

        def one(i, carry):
            xx, zz = shift(x, lax.rem(i, 4)), shift(z, i // 4)
            cols = blend(zz * SIDE + xx)
            for m in (0, 1):
                send(mix.at[m, :, cols], target, w_ss.at[k], w_rs.at[k], device(xx, y, zz, m))
            return carry

        lax.fori_loop(1, CHIPS, one, 0)

    for copy in loads[1:5]:
        copy.wait()
    send_weights(0)

    for d in (1, 2, 3):
        send_block(x, z, *along_b(d))
    for e in (1, 3, 2):
        xx, zz = block_of(e, 0)
        wait_bytes(act_block(xx, zz, c), act_rs.at[zz * SIDE + xx])
        for d in (1, 3, 2):
            send_block(xx, zz, *along_b(d))
        share_block(xx, zz)

    for k in range(1, len(CHUNKS)):
        send_weights(k)

    for copy in loads[5:]:
        copy.wait()

    def blend_down(i, carry):
        cols = pl.ds(pl.multiple_of(i * UNITS, 128), UNITS)
        mix[2, :, cols] = mixed(mix[2, :, cols], old[2, :, cols])
        return carry

    lax.fori_loop(0, CHIPS, blend_down, 0)

    def send_down():
        target = dbuf.at[weight_rows(x, z, c), :]
        cols = pl.ds(pl.multiple_of(chip * UNITS, 128), UNITS)
        pltpu.make_async_copy(mix.at[2, :, cols], target, d_rs.at[chip]).start()

        def one(i, carry):
            xx, zz = shift(x, lax.rem(i, 4)), shift(z, i // 4)
            cols = pl.ds(pl.multiple_of((zz * SIDE + xx) * UNITS, 128), UNITS)
            send(mix.at[2, :, cols], target, d_ss, d_rs.at[chip], device(xx, y, zz, c))
            return carry

        lax.fori_loop(1, CHIPS, one, 0)

    def share_down():
        def one(i, carry):
            xx, zz = shift(x, lax.rem(i, 4)), shift(z, i // 4)
            ref = dbuf.at[weight_rows(xx, zz, c), :]
            wait_bytes(ref, d_rs.at[zz * SIDE + xx])
            send(ref, ref, d_ss, d_fs, sibling)
            return carry

        lax.fori_loop(0, CHIPS, one, 0)

    for db in (1, 3, 2):
        for da in (0, 1, 3, 2):
            xx, zz = block_of(da, db)
            wait_bytes(act_block(xx, zz, c), act_rs.at[zz * SIDE + xx])
            share_block(xx, zz)
    wait_bytes(act.at[pl.ds(0, TOKENS // 2), :], act_fs)

    def multiply(k):
        c0, cw = CHUNKS[k]
        cols = pl.ds(c0, cw)
        wait_bytes(wbuf.at[:, cols], w_rs.at[k])

        def one(i, carry):
            d = lax.rem(i + 1, SIDE)
            q = shift(y, d)
            rows = pl.ds(pl.multiple_of(q * QUARTER, QUARTER), QUARTER)
            part[rows, cols] = jnp.dot(act[rows, :], wbuf[:, cols], preferred_element_type=F32).astype(BF16)

            @pl.when(i < 3)
            def _():
                send(part.at[rows, cols], rs.at[i, :, cols], r_ss, r_rs.at[k, i], device(x, q, z, c))

            return carry

        lax.fori_loop(0, SIDE, one, 0)

    def reduce(k):
        c0, cw = CHUNKS[k]
        cols = pl.ds(c0, cw)
        for i in range(3):
            wait_bytes(rs.at[i, :, cols], r_rs.at[k, i])

        def one(j, carry):
            rows = pl.ds(pl.multiple_of(j * BLOCK, BLOCK), BLOCK)
            total = part[pl.ds(pl.multiple_of(y * QUARTER + j * BLOCK, BLOCK), BLOCK), cols].astype(F32)
            for i in range(3):
                total = total + rs[i, rows, cols].astype(F32)
            xs[rows, cols] = total
            return carry

        lax.fori_loop(0, SIDE, one, 0)
        for j in (0, 1):
            rows = pl.ds(pl.multiple_of((2 * j + 1 - c) * BLOCK, BLOCK), BLOCK)
            send(xs.at[rows, cols], xr.at[pl.ds(j * BLOCK, BLOCK), cols], x_ss, x_rs.at[k], sibling)

    def activate(k):
        c0, cw = CHUNKS[k]
        cols = pl.ds(c0, cw)
        wait_bytes(xr.at[:, cols], x_rs.at[k])
        for j in (0, 1):
            own = xs[pl.ds(pl.multiple_of((2 * j + c) * BLOCK, BLOCK), BLOCK), cols]
            other = xr[pl.ds(j * BLOCK, BLOCK), cols]
            gate, up = jnp.where(first, own, other), jnp.where(first, other, own)
            hid[pl.ds(pl.multiple_of((y * 2 + j) * BLOCK, BLOCK), BLOCK), cols] = (jax.nn.silu(gate) * up).astype(BF16)
        ref = hid.at[pl.ds(pl.multiple_of(y * 2 * BLOCK, 2 * BLOCK), 2 * BLOCK), cols]
        for d in (1, 2, 3):
            send(ref, ref, h_ss, h_rs.at[k, d - 1], device(x, shift(y, d), z, c))

    multiply(0)
    multiply(1)
    reduce(0)
    multiply(2)
    send_down()
    activate(0)
    reduce(1)
    activate(1)
    reduce(2)
    activate(2)
    share_down()
    wait_bytes(dbuf.at[pl.ds(0, PLANE // 2), :], d_fs)
    for k, (c0, cw) in enumerate(CHUNKS):
        for d in (1, 2, 3):
            wait_bytes(hid.at[pl.ds(0, 2 * BLOCK), pl.ds(c0, cw)], h_rs.at[k, d - 1])

    def project(n, carry):
        tile = dbuf[pl.ds(pl.multiple_of(n * 256, 256), 256), :]
        made = lax.dot_general(hid[...], tile, (((1,), (1,)), ((), ())), preferred_element_type=F32).astype(BF16)
        cols = pl.ds(pl.multiple_of(lax.rem(n, 4) * 256, 256), 256)
        for zz in range(SIDE):
            for xh in range(2):
                xx = xh * 2 + n // 4
                a, b = jnp.where(first, zz, xx), jnp.where(first, xx, zz)
                ob[a, b, :, cols] = made[(zz * 2 + xh) * BLOCK : (zz * 2 + xh + 1) * BLOCK]
        return carry

    lax.fori_loop(0, 8, project, 0)
    a, b = jnp.where(first, z, x), jnp.where(first, x, z)
    for d in (1, 2, 3):
        send(ob.at[shift(a, d)], o1.at[d - 1], o1_ss, o1_rs.at[d - 1], device(along_b(d)[0], y, along_b(d)[1], c))
    for i in range(3):
        wait_bytes(o1.at[i], o1_rs.at[i])
    for d in (1, 2, 3, 0):
        bb = shift(b, d)
        total = ob[a, bb].astype(F32)
        for i in range(3):
            total = total + o1[i, bb].astype(F32)
        if d:
            o2s[d - 1] = total.astype(BF16)
            to_x, to_z = along_a(d)
            send(o2s.at[d - 1], o2.at[d - 1], o2_ss, o2_rs.at[d - 1], device(to_x, y, to_z, c))
    for i in range(3):
        wait_bytes(o2.at[i], o2_rs.at[i])
        total = total + o2[i].astype(F32)
    out[...] = total.astype(BF16)

    wait_bytes(act.at[pl.ds(0, 31 * ROWS), :], act_ss)
    for k, (c0, cw) in enumerate(CHUNKS):
        wait_bytes(wbuf.at[pl.ds(0, 31 * ROWS), pl.ds(c0, cw)], w_ss.at[k])
    wait_bytes(dbuf.at[pl.ds(0, 31 * ROWS), :], d_ss)
    wait_bytes(part.at[pl.ds(0, 3 * QUARTER), :], r_ss)
    wait_bytes(xr, x_ss)
    wait_bytes(hid.at[pl.ds(0, 6 * BLOCK), :], h_ss)
    wait_bytes(o1, o1_ss)
    wait_bytes(o2, o2_ss)


def per_device(activ, policy_gate, policy_up, policy_down, old_gate, old_up, old_down):
    sem = pltpu.SemaphoreType.DMA
    n = len(CHUNKS)
    return pl.pallas_call(
        kernel,
        name="layer",
        out_shape=jax.ShapeDtypeStruct((BLOCK, FEATS), BF16),
        in_specs=[pl.BlockSpec(memory_space=pl.ANY)] * 7,
        out_specs=pl.BlockSpec(memory_space=pltpu.VMEM),
        scratch_shapes=[
            pltpu.VMEM((3, ROWS, CHIPS * UNITS), BF16),
            pltpu.VMEM((3, ROWS, CHIPS * UNITS), BF16),
            pltpu.VMEM((TOKENS, PLANE), BF16),
            pltpu.VMEM((PLANE, UNITS), BF16),
            pltpu.VMEM((PLANE, UNITS), BF16),
            pltpu.VMEM((TOKENS, UNITS), BF16),
            pltpu.VMEM((3, QUARTER, UNITS), BF16),
            pltpu.VMEM((QUARTER, UNITS), F32),
            pltpu.VMEM((2 * BLOCK, UNITS), F32),
            pltpu.VMEM((8 * BLOCK, UNITS), BF16),
            pltpu.VMEM((SIDE, SIDE, BLOCK, FEATS), BF16),
            pltpu.VMEM((3, SIDE, BLOCK, FEATS), BF16),
            pltpu.VMEM((3, BLOCK, FEATS), BF16),
            pltpu.VMEM((3, BLOCK, FEATS), BF16),
            sem((7,)),
            sem, sem((CHIPS,)), sem,
            sem((n,)), sem((n,)),
            sem, sem((CHIPS,)), sem,
            sem, sem((n, 3)),
            sem, sem((n,)),
            sem, sem((n, 3)),
            sem, sem((3,)),
            sem, sem((3,)),
        ],
        compiler_params=pltpu.CompilerParams(
            collective_id=0, has_side_effects=True, vmem_limit_bytes=60 << 20
        ),
    )(activ, policy_gate, policy_up, policy_down.T, old_gate, old_up, old_down.T)


def solution(mesh):
    in_specs = (
        P("tp", "fsdp"),
        P(("fsdp", "tp"), None),
        P(("fsdp", "tp"), None),
        P(None, ("fsdp", "tp")),
        P(("fsdp", "tp"), None),
        P(("fsdp", "tp"), None),
        P(None, ("fsdp", "tp")),
    )
    return jax.shard_map(
        per_device, mesh=mesh, in_specs=in_specs, out_specs=P("tp", "fsdp"), check_vma=False
    )
```

time: 452 us -> 173 us (0.38)
  waiting for transfers between devices: 304 us -> 0 us
  Pallas kernels: 0 us -> 171 us
  blocking collectives: 93.7 us -> 0 us
  matrix products: 20.9 us -> 0 us
  between operations: 13.2 us -> 0.01 us
  other arithmetic: 9.36 us -> 0 us
  starting transfers between devices: 8.13 us -> 0 us
    reduce_scatter x2 -> x0, waiting for transfers between devices: 229 us -> none  [the longest x1 147 us: per_device(): lax.psum_scatter(partials.astype(jnp.bfloat16), 'fsdp', scatter_dimension...]
    pallas_call x0 -> x1, Pallas kernels: none -> 171 us  [per_device(): pl.pallas_call(kernel, name='layer', out_shape=jax.ShapeDtypeStruct((BLOC...]
    all_to_all x2 -> x0, blocking collectives: 93.7 us -> none  [the longest x1 52.5 us: per_device(): lax.all_to_all(blend(policy_down, old_down), 'tp', split_axis=0, concat_a...]
    all_gather x2 -> x0, waiting for transfers between devices: 47.3 us -> none  [the longest x1 45.3 us: per_device(): lax.all_gather(activate(share_sums, width), 'fsdp', axis=0, tiled=True)]
    all_to_all x1 -> x0, waiting for transfers between devices: 26.9 us -> none  [per_device(): lax.all_to_all(blend(policy_gate, old_gate), 'tp', split_axis=1, concat_a...]
    dot_general x2 -> x0, matrix products: 20.9 us -> none  [the longest x1 12.6 us: per_device(): jnp.dot(lax.all_gather(activ, 'tp', axis=0, tiled=True), paired, preferre...]
    convert_element_type x5 -> x0, other arithmetic: 9.36 us -> none  [the longest x3 7.02 us: blend(): (0.6 * policy.astype(jnp.float32) + 0.4 * older.astype(jnp.float32)).asty...]
    all_to_all x1 -> x0, starting transfers between devices: 8.01 us -> none  [per_device(): lax.all_to_all(blend(policy_gate, old_gate), 'tp', split_axis=1, concat_a...]
  transfers between devices with their start and end apart: 5 -> 0, of which waited for: 5 -> 0; matrix products, arithmetic and copies ran while one was open for 2% -> 0% of each run, Pallas kernels for 0% -> 0%
where the time goes in v1:
time: 173 us
  Pallas kernels  171 us (99%)
    pallas_call x1, Pallas kernels, per_device(): pl.pallas_call(kernel, name='layer', out_shape=jax.ShapeDtypeStruct((BLOC...  171 us

profile of v1, /device:TPU:0, one launch (start us, length us, event | category | flops | bytes accessed | tf_op | source)
XLA Modules:
  0.0 172.7 jit_solution(5181828764653376893)
XLA Ops:
  0.0 171.0 %layer.1 = bf16[128,1024]{1,0:T(8,128)(2,1)} custom-call(bf16[128,1024]{1,0:T(8,128)(2,1)} %act_in.1, bf16[64,14336]{1,0:T(8,128)(2,1)} %pg_in.1, bf16[64,14336]{1,0:T(8,128)(2,1)} %pu_in.1, bf16[64,14336]{1,0:T(8,128)(2,1)} %bitcast.2, bf16[64,14336]{1,0:T(8,128)(2,1)} %og_in.1, bf16[64,14336]{1,0:T(8,128)(2,1)} %ou_in.1, bf16[64,14336]{1,0:T(8,128)(2,1)} %bitcast.3), custom_call_target="tpu_custom_call" | custom-call | tf_op jit(solution)/shard_map/layer/pallas_call | solution.py:307
  171.0 1.7 copy.9

commit v2 on v1

--- a/solution.py
+++ b/solution.py
@@ -17,9 +17,10 @@
 PLANE = 2048
 TOKENS = 2048
 QUARTER = 512
+HALF = 256
 BLOCK = 128
 FEATS = 1024
-CHUNKS = ((0, 256), (256, 256), (512, 384))
+CHUNKS = ((0, 128), (128, 256), (384, 256), (640, 256))
 
 
 def device(x, y, z, c):
@@ -40,9 +41,9 @@
 
 def kernel(
     act_in, pg_in, pu_in, pd_in, og_in, ou_in, od_in, out,
-    mix, old, act, wbuf, dbuf, part, rs, xs, xr, hid, ob, o1, o2s, o2,
+    mix, old, act, wbuf, dbuf, part, rl, rf, xs, xr, hid, ob, o1l, o1f, o2s, o2l, o2f,
     ld, act_ss, act_rs, act_fs, w_ss, w_rs, d_ss, d_rs, d_fs,
-    r_ss, r_rs, x_ss, x_rs, h_ss, h_rs, o1_ss, o1_rs, o2_ss, o2_rs,
+    r_ss, r_rl, r_rf, x_ss, x_rs, h_ss, h_rs, h_ro, o1_ss, o1_rl, o1_rf, o2_ss, o2_rl, o2_rf,
 ):
     f, t = lax.axis_index("fsdp"), lax.axis_index("tp")
     y, x_lo = f // 2, lax.rem(f, 2)
@@ -100,18 +101,29 @@
     def block_of(da, db):
         return jnp.where(first, shift(x, da), shift(x, db)), jnp.where(first, shift(z, db), shift(z, da))
 
-    def send_block(xx, zz, to_x, to_z):
+    def send_block(xx, zz, to, half=None):
         ref = act_block(xx, zz, c)
-        send(ref, ref, act_ss, act_rs.at[zz * SIDE + xx], device(to_x, y, to_z, c))
+        if half is not None:
+            ref = ref.at[pl.ds(half * ROWS, ROWS), :]
+        send(ref, ref, act_ss, act_rs.at[zz * SIDE + xx], device(to[0], y, to[1], c))
 
     def share_block(xx, zz):
         ref = act_block(xx, zz, c)
         send(ref, ref, act_ss, act_fs, sibling)
 
+    def await_block(da, db):
+        xx, zz = block_of(da, db)
+        wait_bytes(act_block(xx, zz, c), act_rs.at[zz * SIDE + xx])
+        return xx, zz
+
     loads[0].wait()
-    for d in (1, 3, 2):
-        send_block(x, z, *along_a(d))
+    for d in (1, 3):
+        send_block(x, z, along_a(d))
+        send_block(x, z, along_b(d))
     share_block(x, z)
+
+    def around(i):
+        return shift(x, lax.rem(i, SIDE)), shift(z, lax.rem(i // SIDE + i, SIDE))
 
     def send_weights(k):
         c0, cw = CHUNKS[k]
@@ -128,7 +140,7 @@
         send(mix.at[1 - c, :, own], target, w_ss.at[k], w_rs.at[k], sibling)
 
         def one(i, carry):
-            xx, zz = shift(x, lax.rem(i, 4)), shift(z, i // 4)
+            xx, zz = around(i)
             cols = blend(zz * SIDE + xx)
             for m in (0, 1):
                 send(mix.at[m, :, cols], target, w_ss.at[k], w_rs.at[k], device(xx, y, zz, m))
@@ -140,17 +152,20 @@
         copy.wait()
     send_weights(0)
 
-    for d in (1, 2, 3):
-        send_block(x, z, *along_b(d))
-    for e in (1, 3, 2):
-        xx, zz = block_of(e, 0)
-        wait_bytes(act_block(xx, zz, c), act_rs.at[zz * SIDE + xx])
-        for d in (1, 3, 2):
-            send_block(xx, zz, *along_b(d))
+    for s, da in ((0, 3), (1, 1), (None, 2)):
+        xx, zz = await_block(da, 0)
+        if s is not None:
+            send_block(xx, zz, along_a((1, 3)[s]), s)
+        for d in (1, 3):
+            send_block(xx, zz, along_b(d))
         share_block(xx, zz)
-
-    for k in range(1, len(CHUNKS)):
-        send_weights(k)
+    for da in (0, 3, 1, 2):
+        for s, db in ((0, 3), (1, 1)):
+            xx, zz = await_block(da, db)
+            send_block(xx, zz, along_b((1, 3)[s]), s)
+            share_block(xx, zz)
+
+    send_weights(1)
 
     for copy in loads[5:]:
         copy.wait()
@@ -168,7 +183,7 @@
         pltpu.make_async_copy(mix.at[2, :, cols], target, d_rs.at[chip]).start()
 
         def one(i, carry):
-            xx, zz = shift(x, lax.rem(i, 4)), shift(z, i // 4)
+            xx, zz = around(i)
             cols = pl.ds(pl.multiple_of((zz * SIDE + xx) * UNITS, 128), UNITS)
             send(mix.at[2, :, cols], target, d_ss, d_rs.at[chip], device(xx, y, zz, c))
             return carry
@@ -177,7 +192,7 @@
 
     def share_down():
         def one(i, carry):
-            xx, zz = shift(x, lax.rem(i, 4)), shift(z, i // 4)
+            xx, zz = around(i)
             ref = dbuf.at[weight_rows(xx, zz, c), :]
             wait_bytes(ref, d_rs.at[zz * SIDE + xx])
             send(ref, ref, d_ss, d_fs, sibling)
@@ -185,44 +200,61 @@
 
         lax.fori_loop(0, CHIPS, one, 0)
 
-    for db in (1, 3, 2):
-        for da in (0, 1, 3, 2):
-            xx, zz = block_of(da, db)
-            wait_bytes(act_block(xx, zz, c), act_rs.at[zz * SIDE + xx])
-            share_block(xx, zz)
+    for da in (0, 3, 1, 2):
+        share_block(*await_block(da, 2))
     wait_bytes(act.at[pl.ds(0, TOKENS // 2), :], act_fs)
 
-    def multiply(k):
+    def half_of(q, s):
+        return pl.ds(pl.multiple_of(q * QUARTER + s * HALF, HALF), HALF)
+
+    def multiply(k, *then):
         c0, cw = CHUNKS[k]
         cols = pl.ds(c0, cw)
         wait_bytes(wbuf.at[:, cols], w_rs.at[k])
+        for act_now in then:
+            act_now()
 
         def one(i, carry):
-            d = lax.rem(i + 1, SIDE)
-            q = shift(y, d)
+            q = shift(y, jnp.where(i == 0, 2, jnp.where(i == 3, 0, 2 * i - 1)))
             rows = pl.ds(pl.multiple_of(q * QUARTER, QUARTER), QUARTER)
             part[rows, cols] = jnp.dot(act[rows, :], wbuf[:, cols], preferred_element_type=F32).astype(BF16)
 
-            @pl.when(i < 3)
+            @pl.when(i == 0)
             def _():
-                send(part.at[rows, cols], rs.at[i, :, cols], r_ss, r_rs.at[k, i], device(x, q, z, c))
+                for s, d in ((0, 1), (1, 3)):
+                    send(part.at[half_of(q, s), cols], rl.at[s, :, cols], r_ss, r_rl.at[k, s], device(x, shift(y, d), z, c))
+
+            for s in (0, 1):
+
+                @pl.when(i == s + 1)
+                def _():
+                    o = 1 - s
+                    send(part.at[half_of(q, o), cols], rf.at[s, pl.ds(o * HALF, HALF), cols], r_ss, r_rf.at[k, s], device(x, q, z, c))
 
             return carry
 
         lax.fori_loop(0, SIDE, one, 0)
 
+    def relay(k):
+        c0, cw = CHUNKS[k]
+        cols = pl.ds(c0, cw)
+        for s, d in ((0, 1), (1, 3)):
+            q = shift(y, d)
+            rows = half_of(q, s)
+            wait_bytes(rl.at[s, :, cols], r_rl.at[k, s])
+            part[rows, cols] = (part[rows, cols].astype(F32) + rl[s, :, cols].astype(F32)).astype(BF16)
+            send(part.at[rows, cols], rf.at[s, pl.ds(s * HALF, HALF), cols], r_ss, r_rf.at[k, s], device(x, q, z, c))
+
     def reduce(k):
         c0, cw = CHUNKS[k]
         cols = pl.ds(c0, cw)
-        for i in range(3):
-            wait_bytes(rs.at[i, :, cols], r_rs.at[k, i])
+        for s in (0, 1):
+            wait_bytes(rf.at[s, :, cols], r_rf.at[k, s])
 
         def one(j, carry):
             rows = pl.ds(pl.multiple_of(j * BLOCK, BLOCK), BLOCK)
             total = part[pl.ds(pl.multiple_of(y * QUARTER + j * BLOCK, BLOCK), BLOCK), cols].astype(F32)
-            for i in range(3):
-                total = total + rs[i, rows, cols].astype(F32)
-            xs[rows, cols] = total
+            xs[rows, cols] = total + rf[0, rows, cols].astype(F32) + rf[1, rows, cols].astype(F32)
             return carry
 
         lax.fori_loop(0, SIDE, one, 0)
@@ -239,55 +271,120 @@
             other = xr[pl.ds(j * BLOCK, BLOCK), cols]
             gate, up = jnp.where(first, own, other), jnp.where(first, other, own)
             hid[pl.ds(pl.multiple_of((y * 2 + j) * BLOCK, BLOCK), BLOCK), cols] = (jax.nn.silu(gate) * up).astype(BF16)
-        ref = hid.at[pl.ds(pl.multiple_of(y * 2 * BLOCK, 2 * BLOCK), 2 * BLOCK), cols]
-        for d in (1, 2, 3):
-            send(ref, ref, h_ss, h_rs.at[k, d - 1], device(x, shift(y, d), z, c))
-
-    multiply(0)
-    multiply(1)
+        ref = hid.at[pl.ds(pl.multiple_of(y * HALF, HALF), HALF), cols]
+        for s, d in ((0, 1), (1, 3)):
+            send(ref, ref, h_ss, h_rs.at[k, s], device(x, shift(y, d), z, c))
+
+    def forward(k):
+        c0, cw = CHUNKS[k]
+        cols = pl.ds(c0, cw)
+        for s, d in ((0, 1), (1, 3)):
+            q = shift(y, SIDE - d)
+            wait_bytes(hid.at[pl.ds(pl.multiple_of(q * HALF, HALF), HALF), cols], h_rs.at[k, s])
+            ref = hid.at[pl.ds(pl.multiple_of(q * HALF + s * BLOCK, BLOCK), BLOCK), cols]
+            send(ref, ref, h_ss, h_ro.at[k], device(x, shift(y, d), z, c))
+
+    multiply(0, lambda: send_weights(2))
+    relay(0)
+    multiply(1, lambda: send_weights(3))
     reduce(0)
+    relay(1)
+    activate(0)
     multiply(2)
-    send_down()
-    activate(0)
     reduce(1)
+    forward(0)
+    relay(2)
     activate(1)
+    multiply(3, send_down)
     reduce(2)
+    forward(1)
+    relay(3)
     activate(2)
+    reduce(3)
+    forward(2)
+    activate(3)
+    forward(3)
     share_down()
     wait_bytes(dbuf.at[pl.ds(0, PLANE // 2), :], d_fs)
     for k, (c0, cw) in enumerate(CHUNKS):
-        for d in (1, 2, 3):
-            wait_bytes(hid.at[pl.ds(0, 2 * BLOCK), pl.ds(c0, cw)], h_rs.at[k, d - 1])
-
-    def project(n, carry):
-        tile = dbuf[pl.ds(pl.multiple_of(n * 256, 256), 256), :]
-        made = lax.dot_general(hid[...], tile, (((1,), (1,)), ((), ())), preferred_element_type=F32).astype(BF16)
-        cols = pl.ds(pl.multiple_of(lax.rem(n, 4) * 256, 256), 256)
-        for zz in range(SIDE):
-            for xh in range(2):
-                xx = xh * 2 + n // 4
-                a, b = jnp.where(first, zz, xx), jnp.where(first, xx, zz)
-                ob[a, b, :, cols] = made[(zz * 2 + xh) * BLOCK : (zz * 2 + xh + 1) * BLOCK]
-        return carry
-
-    lax.fori_loop(0, 8, project, 0)
+        wait_bytes(hid.at[pl.ds(0, HALF), pl.ds(c0, cw)], h_ro.at[k])
+
     a, b = jnp.where(first, z, x), jnp.where(first, x, z)
-    for d in (1, 2, 3):
-        send(ob.at[shift(a, d)], o1.at[d - 1], o1_ss, o1_rs.at[d - 1], device(along_b(d)[0], y, along_b(d)[1], c))
-    for i in range(3):
-        wait_bytes(o1.at[i], o1_rs.at[i])
-    for d in (1, 2, 3, 0):
-        bb = shift(b, d)
-        total = ob[a, bb].astype(F32)
-        for i in range(3):
-            total = total + o1[i, bb].astype(F32)
-        if d:
-            o2s[d - 1] = total.astype(BF16)
-            to_x, to_z = along_a(d)
-            send(o2s.at[d - 1], o2.at[d - 1], o2_ss, o2_rs.at[d - 1], device(to_x, y, to_z, c))
-    for i in range(3):
-        wait_bytes(o2.at[i], o2_rs.at[i])
-        total = total + o2[i].astype(F32)
+    first_to = [device(along_b(d)[0], y, along_b(d)[1], c) for d in (1, 3)]
+    second_to = [device(along_a(d)[0], y, along_a(d)[1], c) for d in (1, 3)]
+    ends = pl.ds(0, ROWS), pl.ds(ROWS, ROWS)
+
+    def product(rows, n, width):
+        tile = dbuf[pl.ds(pl.multiple_of(n * width, width), width), :]
+        return lax.dot_general(rows, tile, (((1,), (1,)), ((), ())), preferred_element_type=F32).astype(BF16)
+
+    def project(j):
+        to = shift(b, (2, 1, 3, 0)[j])
+
+        @pl.when(first)
+        def _():
+            rows = jnp.concatenate(
+                [hid[pl.ds(pl.multiple_of((i * 2 + to // 2) * BLOCK, BLOCK), BLOCK), :] for i in range(SIDE)], axis=0
+            )
+
+            def one(n, carry):
+                made = product(rows, lax.rem(to, 2) * 2 + n, 512)
+                for i in range(SIDE):
+                    ob[j, i, :, pl.ds(pl.multiple_of(n * 512, 512), 512)] = made[i * BLOCK : (i + 1) * BLOCK]
+                return carry
+
+            lax.fori_loop(0, 2, one, 0)
+
+        @pl.when(c == 1)
+        def _():
+            def one(n, carry):
+                made = product(hid[pl.ds(pl.multiple_of(to * HALF, HALF), HALF), :], n, FEATS)
+                for h in (0, 1):
+                    ob[j, h * 2 + n] = made[h * BLOCK : (h + 1) * BLOCK]
+                return carry
+
+            lax.fori_loop(0, 2, one, 0)
+
+        for s, d in ((0, 1), (1, 3)):
+            send(ob.at[j, shift(a, 2), ends[s]], o1l.at[j, s], o1_ss, o1_rl.at[j, s], first_to[s])
+        for s, d in ((0, 1), (1, 3)):
+            send(ob.at[j, shift(a, d), ends[1 - s]], o1f.at[j, s, ends[1 - s]], o1_ss, o1_rf.at[j, s], first_to[s])
+
+    def pass_on(j):
+        for s, d in ((0, 1), (1, 3)):
+            i = shift(a, d)
+            wait_bytes(o1l.at[j, s], o1_rl.at[j, s])
+            ob[j, i, ends[s]] = (ob[j, i, ends[s]].astype(F32) + o1l[j, s].astype(F32)).astype(BF16)
+            send(ob.at[j, i, ends[s]], o1f.at[j, s, ends[s]], o1_ss, o1_rf.at[j, s], first_to[s])
+
+    def added(j):
+        for s in (0, 1):
+            wait_bytes(o1f.at[j, s], o1_rf.at[j, s])
+        return ob[j, a].astype(F32) + o1f[j, 0].astype(F32) + o1f[j, 1].astype(F32)
+
+    project(0)
+    project(1)
+    project(2)
+    pass_on(0)
+    project(3)
+    pass_on(1)
+    o2s[0] = added(0).astype(BF16)
+    for s in (0, 1):
+        send(o2s.at[0, ends[s]], o2l.at[s], o2_ss, o2_rl.at[s], second_to[s])
+    pass_on(2)
+    o2s[1] = added(1).astype(BF16)
+    send(o2s.at[1, ends[1]], o2f.at[0, ends[1]], o2_ss, o2_rf.at[0], second_to[0])
+    pass_on(3)
+    o2s[2] = added(2).astype(BF16)
+    send(o2s.at[2, ends[0]], o2f.at[1, ends[0]], o2_ss, o2_rf.at[1], second_to[1])
+    for s in (0, 1):
+        wait_bytes(o2l.at[s], o2_rl.at[s])
+        o2s[s + 1, ends[s]] = (o2s[s + 1, ends[s]].astype(F32) + o2l[s].astype(F32)).astype(BF16)
+        send(o2s.at[s + 1, ends[s]], o2f.at[s, ends[s]], o2_ss, o2_rf.at[s], second_to[s])
+    total = added(3)
+    for s in (0, 1):
+        wait_bytes(o2f.at[s], o2_rf.at[s])
+        total = total + o2f[s].astype(F32)
     out[...] = total.astype(BF16)
 
     wait_bytes(act.at[pl.ds(0, 31 * ROWS), :], act_ss)
@@ -297,8 +394,8 @@
     wait_bytes(part.at[pl.ds(0, 3 * QUARTER), :], r_ss)
     wait_bytes(xr, x_ss)
     wait_bytes(hid.at[pl.ds(0, 6 * BLOCK), :], h_ss)
-    wait_bytes(o1, o1_ss)
-    wait_bytes(o2, o2_ss)
+    wait_bytes(ob.at[pl.ds(0, 3)], o1_ss)
+    wait_bytes(o2s, o2_ss)
 
 
 def per_device(activ, policy_gate, policy_up, policy_down, old_gate, old_up, old_down):
@@ -317,23 +414,26 @@
             pltpu.VMEM((PLANE, UNITS), BF16),
             pltpu.VMEM((PLANE, UNITS), BF16),
             pltpu.VMEM((TOKENS, UNITS), BF16),
-            pltpu.VMEM((3, QUARTER, UNITS), BF16),
+            pltpu.VMEM((2, HALF, UNITS), BF16),
+            pltpu.VMEM((2, QUARTER, UNITS), BF16),
             pltpu.VMEM((QUARTER, UNITS), F32),
             pltpu.VMEM((2 * BLOCK, UNITS), F32),
             pltpu.VMEM((8 * BLOCK, UNITS), BF16),
             pltpu.VMEM((SIDE, SIDE, BLOCK, FEATS), BF16),
-            pltpu.VMEM((3, SIDE, BLOCK, FEATS), BF16),
+            pltpu.VMEM((SIDE, 2, ROWS, FEATS), BF16),
+            pltpu.VMEM((SIDE, 2, BLOCK, FEATS), BF16),
             pltpu.VMEM((3, BLOCK, FEATS), BF16),
-            pltpu.VMEM((3, BLOCK, FEATS), BF16),
+            pltpu.VMEM((2, ROWS, FEATS), BF16),
+            pltpu.VMEM((2, BLOCK, FEATS), BF16),
             sem((7,)),
             sem, sem((CHIPS,)), sem,
             sem((n,)), sem((n,)),
             sem, sem((CHIPS,)), sem,
-            sem, sem((n, 3)),
+            sem, sem((n, 2)), sem((n, 2)),
             sem, sem((n,)),
-            sem, sem((n, 3)),
-            sem, sem((3,)),
-            sem, sem((3,)),
+            sem, sem((n, 2)), sem((n,)),
+            sem, sem((SIDE, 2)), sem((SIDE, 2)),
+            sem, sem((2,)), sem((2,)),
         ],
         compiler_params=pltpu.CompilerParams(
             collective_id=0, has_side_effects=True, vmem_limit_bytes=60 << 20

time: 173 us -> 135 us (0.78)
  Pallas kernels: 171 us -> 133 us
    pallas_call x1, Pallas kernels: 171 us -> 133 us  [per_device(): pl.pallas_call(kernel, name='layer', out_shape=jax.ShapeDtypeStruct((BLOC...]
where the time goes in v2:
time: 135 us
  Pallas kernels  133 us (99%)
  local copies, waits for them, and re-layouts  1.67 us (1%)
    pallas_call x1, Pallas kernels, per_device(): pl.pallas_call(kernel, name='layer', out_shape=jax.ShapeDtypeStruct((BLOC...  133 us

profile of v2, /device:TPU:0, one launch (start us, length us, event | category | flops | bytes accessed | tf_op | source)
XLA Modules:
  0.0 134.9 jit_solution(18321556428439405883)
XLA Ops:
  0.0 133.2 %layer.1 = bf16[128,1024]{1,0:T(8,128)(2,1)} custom-call(bf16[128,1024]{1,0:T(8,128)(2,1)} %act_in.1, bf16[64,14336]{1,0:T(8,128)(2,1)} %pg_in.1, bf16[64,14336]{1,0:T(8,128)(2,1)} %pu_in.1, bf16[64,14336]{1,0:T(8,128)(2,1)} %bitcast.2, bf16[64,14336]{1,0:T(8,128)(2,1)} %og_in.1, bf16[64,14336]{1,0:T(8,128)(2,1)} %ou_in.1, bf16[64,14336]{1,0:T(8,128)(2,1)} %bitcast.3), custom_call_target="tpu_custom_call" | custom-call | tf_op jit(solution)/shard_map/layer/pallas_call | solution.py:404
  133.3 1.7 %copy.9 = bf16[128,1024]{1,0:T(8,128)(2,1)} copy(bf16[128,1024]{1,0:T(8,128)(2,1)} %layer.1) | data formatting | bytes 524288

commit v3 on v2

--- a/solution.py
+++ b/solution.py
@@ -20,7 +20,9 @@
 HALF = 256
 BLOCK = 128
 FEATS = 1024
-CHUNKS = ((0, 128), (128, 256), (384, 256), (640, 256))
+CHUNKS = ((0, 128), (128, 128), (256, 128), (384, 128), (512, 128), (640, 128), (768, 128))
+
+DOWN_PARTS = ((1, 8), (8, 16))
 
 
 def device(x, y, z, c):
@@ -42,7 +44,7 @@
 def kernel(
     act_in, pg_in, pu_in, pd_in, og_in, ou_in, od_in, out,
     mix, old, act, wbuf, dbuf, part, rl, rf, xs, xr, hid, ob, o1l, o1f, o2s, o2l, o2f,
-    ld, act_ss, act_rs, act_fs, w_ss, w_rs, d_ss, d_rs, d_fs,
+    known, ld, act_ss, act_rs, act_fs, w_ss, w_rs, d_ss, d_rs, d_fs,
     r_ss, r_rl, r_rf, x_ss, x_rs, h_ss, h_rs, h_ro, o1_ss, o1_rl, o1_rf, o2_ss, o2_rl, o2_rf,
 ):
     f, t = lax.axis_index("fsdp"), lax.axis_index("tp")
@@ -81,16 +83,12 @@
         copy.start()
 
     barrier = pltpu.get_barrier_semaphore()
-
-    def greet(i, carry):
-        to = device(shift(x, lax.rem(i // 2, 4)), y, shift(z, i // 8), lax.rem(c + i, 2))
+    ring_x = [device(shift(x, d), y, z, c) for d in (1, 2, 3)]
+    ring_z = [device(x, y, shift(z, d), c) for d in (1, 2, 3)]
+    next_y = [device(x, shift(y, d), z, c) for d in (1, 3)]
+    for to in (*ring_x, *ring_z, *next_y, sibling):
         pl.semaphore_signal(barrier, inc=1, device_id=to, device_id_type=MESH)
-        return carry
-
-    lax.fori_loop(1, 32, greet, 0)
-    for d in (1, 2, 3):
-        pl.semaphore_signal(barrier, inc=1, device_id=device(x, shift(y, d), z, c), device_id_type=MESH)
-    pl.semaphore_wait(barrier, 34)
+    pl.semaphore_wait(barrier, 9)
 
     def along_a(d):
         return jnp.where(first, shift(x, d), x), jnp.where(first, z, shift(z, d))
@@ -122,35 +120,60 @@
         send_block(x, z, along_b(d))
     share_block(x, z)
 
+    for to in ring_z:
+        pl.semaphore_signal(known.at[0], inc=1, device_id=to, device_id_type=MESH)
+    pl.semaphore_wait(known.at[0], 3)
+    pl.semaphore_signal(known.at[1], inc=1, device_id=sibling, device_id_type=MESH)
+    pl.semaphore_wait(known.at[1], 1)
+
     def around(i):
-        return shift(x, lax.rem(i, SIDE)), shift(z, lax.rem(i // SIDE + i, SIDE))
-
-    def send_weights(k):
+        u, v = lax.rem(i, SIDE), lax.rem(i // SIDE + i, SIDE)
+        return shift(x, jnp.where(first, u, v)), shift(z, jnp.where(first, v, u))
+
+    def columns(p, c0, cw):
+        return pl.ds(pl.multiple_of(p * UNITS + c0, 128), cw)
+
+    def blend(m, p, c0, cw):
+        cols = columns(p, c0, cw)
+        mix[m, :, cols] = mixed(mix[m, :, cols], old[m, :, cols])
+
+    def send_weights(k, then=None):
         c0, cw = CHUNKS[k]
         target = wbuf.at[weight_rows(x, z, c), pl.ds(c0, cw)]
-
-        def blend(p):
-            cols = pl.ds(pl.multiple_of(p * UNITS + c0, 128), cw)
-            for m in (0, 1):
-                mix[m, :, cols] = mixed(mix[m, :, cols], old[m, :, cols])
-            return cols
-
-        own = blend(chip)
+        if then:
+            then(chip)
+        own = columns(chip, c0, cw)
         pltpu.make_async_copy(mix.at[c, :, own], target, w_rs.at[k]).start()
         send(mix.at[1 - c, :, own], target, w_ss.at[k], w_rs.at[k], sibling)
 
         def one(i, carry):
             xx, zz = around(i)
-            cols = blend(zz * SIDE + xx)
+            p = zz * SIDE + xx
+            if then:
+                then(p)
             for m in (0, 1):
-                send(mix.at[m, :, cols], target, w_ss.at[k], w_rs.at[k], device(xx, y, zz, m))
+                send(mix.at[m, :, columns(p, c0, cw)], target, w_ss.at[k], w_rs.at[k], device(xx, y, zz, m))
             return carry
 
         lax.fori_loop(1, CHIPS, one, 0)
+
+    def blend_first(p):
+        for m in (0, 1):
+            blend(m, p, *CHUNKS[0])
+
+    def blend_rest(p, carry):
+        for m in (0, 1):
+            blend(m, p, CHUNKS[0][1], UNITS - CHUNKS[0][1])
+        return carry
+
+    def blend_down(p, carry):
+        blend(2, p, 0, UNITS)
+        return carry
 
     for copy in loads[1:5]:
         copy.wait()
-    send_weights(0)
+    send_weights(0, blend_first)
+    lax.fori_loop(0, CHIPS, blend_rest, 0)
 
     for s, da in ((0, 3), (1, 1), (None, 2)):
         xx, zz = await_block(da, 0)
@@ -166,29 +189,23 @@
             share_block(xx, zz)
 
     send_weights(1)
+    send_weights(2)
 
     for copy in loads[5:]:
         copy.wait()
-
-    def blend_down(i, carry):
-        cols = pl.ds(pl.multiple_of(i * UNITS, 128), UNITS)
-        mix[2, :, cols] = mixed(mix[2, :, cols], old[2, :, cols])
-        return carry
-
     lax.fori_loop(0, CHIPS, blend_down, 0)
 
-    def send_down():
+    def send_down(part):
         target = dbuf.at[weight_rows(x, z, c), :]
-        cols = pl.ds(pl.multiple_of(chip * UNITS, 128), UNITS)
-        pltpu.make_async_copy(mix.at[2, :, cols], target, d_rs.at[chip]).start()
+        if part == 0:
+            pltpu.make_async_copy(mix.at[2, :, columns(chip, 0, UNITS)], target, d_rs.at[chip]).start()
 
         def one(i, carry):
             xx, zz = around(i)
-            cols = pl.ds(pl.multiple_of((zz * SIDE + xx) * UNITS, 128), UNITS)
-            send(mix.at[2, :, cols], target, d_ss, d_rs.at[chip], device(xx, y, zz, c))
+            send(mix.at[2, :, columns(zz * SIDE + xx, 0, UNITS)], target, d_ss, d_rs.at[chip], device(xx, y, zz, c))
             return carry
 
-        lax.fori_loop(1, CHIPS, one, 0)
+        lax.fori_loop(*DOWN_PARTS[part], one, 0)
 
     def share_down():
         def one(i, carry):
@@ -211,8 +228,8 @@
         c0, cw = CHUNKS[k]
         cols = pl.ds(c0, cw)
         wait_bytes(wbuf.at[:, cols], w_rs.at[k])
-        for act_now in then:
-            act_now()
+        for step, n in then:
+            step(n)
 
         def one(i, carry):
             q = shift(y, jnp.where(i == 0, 2, jnp.where(i == 3, 0, 2 * i - 1)))
@@ -284,26 +301,41 @@
             ref = hid.at[pl.ds(pl.multiple_of(q * HALF + s * BLOCK, BLOCK), BLOCK), cols]
             send(ref, ref, h_ss, h_ro.at[k], device(x, shift(y, d), z, c))
 
-    multiply(0, lambda: send_weights(2))
+    multiply(0, (send_weights, 3))
+    multiply(1, (send_weights, 4))
     relay(0)
-    multiply(1, lambda: send_weights(3))
+    multiply(2, (send_weights, 5))
+    relay(1)
     reduce(0)
-    relay(1)
+    multiply(3, (send_weights, 6))
+    relay(2)
+    reduce(1)
     activate(0)
-    multiply(2)
-    reduce(1)
+    multiply(4)
+    relay(3)
+    reduce(2)
+    activate(1)
     forward(0)
-    relay(2)
-    activate(1)
-    multiply(3, send_down)
-    reduce(2)
+    multiply(5, (send_down, 0), (send_down, 1))
+    relay(4)
+    reduce(3)
+    activate(2)
     forward(1)
-    relay(3)
-    activate(2)
-    reduce(3)
+    multiply(6)
+    relay(5)
+    reduce(4)
+    activate(3)
     forward(2)
-    activate(3)
+    relay(6)
+    reduce(5)
+    activate(4)
     forward(3)
+    reduce(6)
+    activate(5)
+    forward(4)
+    activate(6)
+    forward(5)
+    forward(6)
     share_down()
     wait_bytes(dbuf.at[pl.ds(0, PLANE // 2), :], d_fs)
     for k, (c0, cw) in enumerate(CHUNKS):
@@ -345,6 +377,7 @@
 
             lax.fori_loop(0, 2, one, 0)
 
+    def emit(j):
         for s, d in ((0, 1), (1, 3)):
             send(ob.at[j, shift(a, 2), ends[s]], o1l.at[j, s], o1_ss, o1_rl.at[j, s], first_to[s])
         for s, d in ((0, 1), (1, 3)):
@@ -362,25 +395,37 @@
             wait_bytes(o1f.at[j, s], o1_rf.at[j, s])
         return ob[j, a].astype(F32) + o1f[j, 0].astype(F32) + o1f[j, 1].astype(F32)
 
+    def finish(j):
+        o2s[j] = added(j).astype(BF16)
+        if j == 0:
+            for s in (0, 1):
+                send(o2s.at[0, ends[s]], o2l.at[s], o2_ss, o2_rl.at[s], second_to[s])
+        else:
+            s = j - 1
+            send(o2s.at[j, ends[1 - s]], o2f.at[s, ends[1 - s]], o2_ss, o2_rf.at[s], second_to[s])
+
+    def finish_far():
+        for s in (0, 1):
+            wait_bytes(o2l.at[s], o2_rl.at[s])
+            o2s[s + 1, ends[s]] = (o2s[s + 1, ends[s]].astype(F32) + o2l[s].astype(F32)).astype(BF16)
+            send(o2s.at[s + 1, ends[s]], o2f.at[s, ends[s]], o2_ss, o2_rf.at[s], second_to[s])
+
     project(0)
+    emit(0)
     project(1)
+    emit(1)
     project(2)
+    emit(2)
     pass_on(0)
     project(3)
+    emit(3)
     pass_on(1)
-    o2s[0] = added(0).astype(BF16)
-    for s in (0, 1):
-        send(o2s.at[0, ends[s]], o2l.at[s], o2_ss, o2_rl.at[s], second_to[s])
+    finish(0)
     pass_on(2)
-    o2s[1] = added(1).astype(BF16)
-    send(o2s.at[1, ends[1]], o2f.at[0, ends[1]], o2_ss, o2_rf.at[0], second_to[0])
+    finish(1)
     pass_on(3)
-    o2s[2] = added(2).astype(BF16)
-    send(o2s.at[2, ends[0]], o2f.at[1, ends[0]], o2_ss, o2_rf.at[1], second_to[1])
-    for s in (0, 1):
-        wait_bytes(o2l.at[s], o2_rl.at[s])
-        o2s[s + 1, ends[s]] = (o2s[s + 1, ends[s]].astype(F32) + o2l[s].astype(F32)).astype(BF16)
-        send(o2s.at[s + 1, ends[s]], o2f.at[s, ends[s]], o2_ss, o2_rf.at[s], second_to[s])
+    finish(2)
+    finish_far()
     total = added(3)
     for s in (0, 1):
         wait_bytes(o2f.at[s], o2_rf.at[s])
@@ -425,6 +470,7 @@
             pltpu.VMEM((3, BLOCK, FEATS), BF16),
             pltpu.VMEM((2, ROWS, FEATS), BF16),
             pltpu.VMEM((2, BLOCK, FEATS), BF16),
+            pltpu.SemaphoreType.REGULAR((2,)),
             sem((7,)),
             sem, sem((CHIPS,)), sem,
             sem((n,)), sem((n,)),

time: 135 us -> 126 us (0.933); the launches traced: 135 us -> 124 us
  Pallas kernels: 133 us -> 123 us
    pallas_call x1, Pallas kernels: 133 us -> 123 us  [per_device(): pl.pallas_call(kernel, name='layer', out_shape=jax.ShapeDtypeStruct((BLOC...]
where the time goes in v3:
time: 126 us; the launch traced here: 124 us
  Pallas kernels  123 us (98%)
  local copies, waits for them, and re-layouts  1.67 us (1%)
    pallas_call x1, Pallas kernels, per_device(): pl.pallas_call(kernel, name='layer', out_shape=jax.ShapeDtypeStruct((BLOC...  123 us

profile of v3, /device:TPU:0, one launch (start us, length us, event | category | flops | bytes accessed | tf_op | source)
XLA Modules:
  0.0 124.4 jit_solution(6145043190705424202)
XLA Ops:
  0.0 122.7 %layer.1 = bf16[128,1024]{1,0:T(8,128)(2,1)} custom-call(bf16[128,1024]{1,0:T(8,128)(2,1)} %act_in.1, bf16[64,14336]{1,0:T(8,128)(2,1)} %pg_in.1, bf16[64,14336]{1,0:T(8,128)(2,1)} %pu_in.1, bf16[64,14336]{1,0:T(8,128)(2,1)} %bitcast.2, bf16[64,14336]{1,0:T(8,128)(2,1)} %og_in.1, bf16[64,14336]{1,0:T(8,128)(2,1)} %ou_in.1, bf16[64,14336]{1,0:T(8,128)(2,1)} %bitcast.3), custom_call_target="tpu_custom_call" | custom-call | tf_op jit(solution)/shard_map/layer/pallas_call | solution.py:449
  122.7 1.7 %copy.9 = bf16[128,1024]{1,0:T(8,128)(2,1)} copy(bf16[128,1024]{1,0:T(8,128)(2,1)} %layer.1) | data formatting | bytes 524288

commit v4 on v3

--- a/solution.py
+++ b/solution.py
@@ -416,15 +416,15 @@
     emit(1)
     project(2)
     emit(2)
+    project(3)
     pass_on(0)
-    project(3)
+    pass_on(1)
+    pass_on(2)
     emit(3)
-    pass_on(1)
     finish(0)
-    pass_on(2)
     finish(1)
+    finish(2)
     pass_on(3)
-    finish(2)
     finish_far()
     total = added(3)
     for s in (0, 1):
@@ -449,7 +449,7 @@
     return pl.pallas_call(
         kernel,
         name="layer",
-        out_shape=jax.ShapeDtypeStruct((BLOCK, FEATS), BF16),
+        out_shape=pltpu.VMEM((BLOCK, FEATS), BF16),
         in_specs=[pl.BlockSpec(memory_space=pl.ANY)] * 7,
         out_specs=pl.BlockSpec(memory_space=pltpu.VMEM),
         scratch_shapes=[

time: 126 us -> 123 us (0.976); the launches traced: 124 us -> 123 us
  no operation moved by 1% of the time
where the time goes in v4:
time: 123 us
  Pallas kernels  122 us (99%)
    pallas_call x1, Pallas kernels, per_device(): pl.pallas_call(kernel, name='layer', out_shape=pltpu.VMEM((BLOCK, FEATS),...  122 us

profile of v4, /device:TPU:0, one launch (start us, length us, event | category | flops | bytes accessed | tf_op | source)
XLA Modules:
  0.0 122.8 jit_solution(1627056214281739478)
XLA Ops:
  0.0 122.1 %layer.1 = bf16[128,1024]{1,0:T(8,128)(2,1)S(1)} custom-call(bf16[128,1024]{1,0:T(8,128)(2,1)} %act_in.1, bf16[64,14336]{1,0:T(8,128)(2,1)} %pg_in.1, bf16[64,14336]{1,0:T(8,128)(2,1)} %pu_in.1, bf16[64,14336]{1,0:T(8,128)(2,1)} %bitcast.2, bf16[64,14336]{1,0:T(8,128)(2,1)} %og_in.1, bf16[64,14336]{1,0:T(8,128)(2,1)} %ou_in.1, bf16[64,14336]{1,0:T(8,128)(2,1)} %bitcast.3), custom_call_target="tpu_custom_call" | custom-call | tf_op jit(solution)/shard_map/layer/pallas_call | solution.py:449
  122.1 0.7 copy.9

commit v5 on v4

--- a/solution.py
+++ b/solution.py
@@ -228,8 +228,6 @@
         c0, cw = CHUNKS[k]
         cols = pl.ds(c0, cw)
         wait_bytes(wbuf.at[:, cols], w_rs.at[k])
-        for step, n in then:
-            step(n)
 
         def one(i, carry):
             q = shift(y, jnp.where(i == 0, 2, jnp.where(i == 3, 0, 2 * i - 1)))
@@ -250,7 +248,10 @@
 
             return carry
 
-        lax.fori_loop(0, SIDE, one, 0)
+        lax.fori_loop(0, 1, one, 0)
+        for step, n in then:
+            step(n)
+        lax.fori_loop(1, SIDE, one, 0)
 
     def relay(k):
         c0, cw = CHUNKS[k]

time: 123 us -> 122 us (level)
  no operation moved by 1% of the time
where the time goes in v5:
time: 122 us
  Pallas kernels  122 us (100%)
    pallas_call x1, Pallas kernels, per_device(): pl.pallas_call(kernel, name='layer', out_shape=pltpu.VMEM((BLOCK, FEATS),...  122 us

profile of v5, /device:TPU:0, one launch (start us, length us, event | category | flops | bytes accessed | tf_op | source)
XLA Modules:
  0.0 122.3 jit_solution(14794743175782642744)
XLA Ops:
  0.0 121.6 %layer.1 = bf16[128,1024]{1,0:T(8,128)(2,1)S(1)} custom-call(bf16[128,1024]{1,0:T(8,128)(2,1)} %act_in.1, bf16[64,14336]{1,0:T(8,128)(2,1)} %pg_in.1, bf16[64,14336]{1,0:T(8,128)(2,1)} %pu_in.1, bf16[64,14336]{1,0:T(8,128)(2,1)} %bitcast.2, bf16[64,14336]{1,0:T(8,128)(2,1)} %og_in.1, bf16[64,14336]{1,0:T(8,128)(2,1)} %ou_in.1, bf16[64,14336]{1,0:T(8,128)(2,1)} %bitcast.3), custom_call_target="tpu_custom_call" | custom-call | tf_op jit(solution)/shard_map/layer/pallas_call | solution.py:450
  121.6 0.7 copy.9

commit v6 on v5

--- a/solution.py
+++ b/solution.py
@@ -248,10 +248,10 @@
 
             return carry
 
-        lax.fori_loop(0, 1, one, 0)
+        lax.fori_loop(0, 2, one, 0)
         for step, n in then:
             step(n)
-        lax.fori_loop(1, SIDE, one, 0)
+        lax.fori_loop(2, SIDE, one, 0)
 
     def relay(k):
         c0, cw = CHUNKS[k]

time: 122 us -> 129 us (1.057)
  Pallas kernels: 122 us -> 128 us
    pallas_call x1, Pallas kernels: 122 us -> 128 us  [per_device(): pl.pallas_call(kernel, name='layer', out_shape=pltpu.VMEM((BLOCK, FEATS),...]
where the time goes in v6:
time: 129 us
  Pallas kernels  128 us (99%)
    pallas_call x1, Pallas kernels, per_device(): pl.pallas_call(kernel, name='layer', out_shape=pltpu.VMEM((BLOCK, FEATS),...  128 us

profile of v6, /device:TPU:0, one launch (start us, length us, event | category | flops | bytes accessed | tf_op | source)
XLA Modules:
  0.0 128.7 jit_solution(11047801952702256667)
XLA Ops:
  0.0 128.0 %layer.1 = bf16[128,1024]{1,0:T(8,128)(2,1)S(1)} custom-call(bf16[128,1024]{1,0:T(8,128)(2,1)} %act_in.1, bf16[64,14336]{1,0:T(8,128)(2,1)} %pg_in.1, bf16[64,14336]{1,0:T(8,128)(2,1)} %pu_in.1, bf16[64,14336]{1,0:T(8,128)(2,1)} %bitcast.2, bf16[64,14336]{1,0:T(8,128)(2,1)} %og_in.1, bf16[64,14336]{1,0:T(8,128)(2,1)} %ou_in.1, bf16[64,14336]{1,0:T(8,128)(2,1)} %bitcast.3), custom_call_target="tpu_custom_call" | custom-call | tf_op jit(solution)/shard_map/layer/pallas_call | solution.py:450
  128.0 0.7 copy.9
